TPU v7x, 32 devices: a whole 2x2x4 slice. The times are simulated.
32 devices in a mesh: users: 8 (over z, x), panel: 4 (over y, core).
Axes of the slice: x: 2, y: 2, z: 4, core: 2. Of those that a mesh axis runs over, the one named last changes fastest.
Arguments:
- user_emb0: float32 [8192, 128], P('users'), may hold values from -6 to 6
- item_base: float32 [4, 1024, 128], P('panel'), may hold values from -6 to 6
- weight_tiles: bfloat16 [64, 128, 128], replicated, may hold values from -0.02734375 to 0.02734375
- blk_user: int32 [8, 4, 384], P('users', 'panel'), may hold values from 0 to 7
- blk_item: int32 [8, 4, 384], P('users', 'panel'), may hold values from 0 to 7
- blk_weight: int32 [8, 4, 384], P('users', 'panel'), may hold values from 0 to 63
Outputs:
- user_out: float32 [8192, 128], P('users')
- item_emb: float32 [4, 1024, 128], P('panel', 'users')
All inputs are finite; a program needn't handle non-finite values.
Results may differ from a plain program's by a relative error of at most 0.0036.
Values may be sent and summed in bfloat16 or wider, within the bound.
A program may use at most 128 MiB of HBM per device.

v0:
```python
import jax
import jax.numpy as jnp
from jax import lax
from jax.sharding import PartitionSpec as P

teleport = 0.2


def item_terms(user_tiles, users, items, weights, weight_tiles, n_items):
    group_size = min(users.shape[0], 128)
    pieces = (
        users.reshape(-1, group_size),
        items.reshape(-1, group_size),
        weights.reshape(-1, group_size),
    )

    def item_add_group(totals, lists):
        tiles = weight_tiles[lists[2]]
        rows = user_tiles[lists[0]]
        products = jnp.einsum("gab,gae->gbe", tiles, rows, preferred_element_type=jnp.float32)
        return (totals + jax.ops.segment_sum(products, lists[1], num_segments=n_items), None)

    start = jnp.zeros((n_items, user_tiles.shape[1], user_tiles.shape[2]), jnp.float32)
    totals, unused = lax.scan(item_add_group, start, pieces)
    return totals


def user_terms(item_tiles, users, items, weights, weight_tiles, n_tiles):
    group_size = min(users.shape[0], 128)
    pieces = (
        users.reshape(-1, group_size),
        items.reshape(-1, group_size),
        weights.reshape(-1, group_size),
    )

    def user_add_group(totals, lists):
        tiles = weight_tiles[lists[2]]
        rows = item_tiles[lists[1]]
        products = jnp.einsum("gab,gbe->gae", tiles, rows, preferred_element_type=jnp.float32)
        return (totals + jax.ops.segment_sum(products, lists[0], num_segments=n_tiles), None)

    start = jnp.zeros((n_tiles, item_tiles.shape[1], item_tiles.shape[2]), jnp.float32)
    totals, unused = lax.scan(user_add_group, start, pieces)
    return totals


def per_device(user_emb0, item_base, weight_tiles, blk_user, blk_item, blk_weight):
    tile_rows = weight_tiles.shape[1]
    width = user_emb0.shape[1]
    n_users = lax.axis_size("users")
    user_tiles = user_emb0.astype(jnp.bfloat16).reshape(-1, tile_rows, width)
    n_user_tiles = user_tiles.shape[0]
    user_list = blk_user.reshape(-1)
    item_list = blk_item.reshape(-1)
    weight_list = blk_weight.reshape(-1)
    partial_value = item_terms(user_tiles, user_list, item_list, weight_list, weight_tiles, n_users)
    partial_flat = partial_value.reshape(n_users * tile_rows, width)
    panel_base = item_base[0]
    position = lax.axis_index("users")
    totals = lax.psum(partial_flat, "users")
    panel_emb = (1.0 - teleport) * totals + teleport * panel_base
    own_emb = lax.dynamic_slice_in_dim(panel_emb, position * tile_rows, tile_rows, 0)
    panel_bf = panel_emb.astype(jnp.bfloat16)
    item_tiles = panel_bf.reshape(n_users, tile_rows, width)
    user_part = user_terms(
        item_tiles, user_list, item_list, weight_list, weight_tiles, n_user_tiles
    )
    user_sum = lax.psum(user_part, "panel")
    user_out = (1.0 - teleport) * user_sum.reshape(-1, width) + teleport * user_emb0
    return (user_out, own_emb[None])


def solution(mesh):
    placed = (
        P("users", None),
        P("panel", None, None),
        P(),
        P("users", "panel", None),
        P("users", "panel", None),
        P("users", "panel", None),
    )
    return jax.shard_map(
        per_device,
        mesh=mesh,
        in_specs=placed,
        out_specs=(P("users", None), P("panel", "users", None)),
        check_vma=False,
    )
```

profile of v0, /device:TPU:0, one launch (start us, length us, event | category | flops | bytes accessed | tf_op | source)
XLA Modules:
  0.0 327.2 jit_solution(5989638884354582941)
XLA Ops:
  7.2 0.0 all-reduce.3.cloned.1.call-start
  7.2 0.7 reduce
  7.9 0.7 reduce.1
  8.6 0.7 reduce.2
  9.3 1.1 convert_element_type.6
  10.4 0.0 copy-start.3
  10.4 99.0 %while.20 = (s32[]{:T(128)}, f32[8,128,128]{2,1,0:T(8,128)S(1)}, s32[3,128]{1,0:T(4,128)S(1)}, s32[3,128]{1,0:T(4,128)S(1)}, bf16[64,128,128]{2,1,0:T(8,128)(2,1...) while((s32[]{:T(128)}, f32[8,128,128]{2,1,0:T(8,128)S(1)}, ...), condition=%wide.region_2.3_spmd, body=%wide.region_0.2_spmd.sunk | while | flops 538970880 | bytes 58734172 | solution.py:24
  10.5 4.7 %gather_fusion = bf16[128,128,128]{2,1,0:T(8,128)(2,1)} fusion(bf16[64,128,128]{2,1,0:T(8,128)(2,1)} %get-tuple-element.226, s32[1024]{0:T(1024)S(1)} %pad_clamp_fusion.8), kind=kCustom, calls=%fused_computation.clone.1 | custom fusion | bytes 8389120 | tf_op jit(solution)/shard_map/while/body/eval_jaxpr/gather | solution.py:18
  15.2 3.0 gather_fusion.1
  18.2 8.2 %fusion.31 = f32[128,128,128]{2,1,0:T(8,128)} fusion(bf16[128,128,128]{2,1,0:T(8,128)(2,1)} %gather_fusion, bf16[128,128,128]{2,1,0:T(8,128)(2,1)} %gather_fusion.1), kind=kOutput, calls=%fused_computation.35.clone.1 | convolution fusion | flops 536870912 | bytes 16777216 | tf_op jit(solution)/shard_map/while/body/eval_jaxpr/gab,gae->gbe/dot_general | solution.py:20
  26.5 17.0 %scatter_fusion = f32[8,128,128]{2,1,0:T(8,128)S(1)} fusion(f32[8,128,128]{2,1,0:T(8,128)S(1)} %get-tuple-element.215, s32[128]{0:T(128)S(1)} %fusion.29, f32[128,128,128]{2,1,0:T(8,128)} %fusion.31), kind=kCustom, calls=%fused_computation.4.clone.1 | custom fusion | flops 2097152 | bytes 25166336 | tf_op jit(solution)/shard_map/while/body/eval_jaxpr/scatter-add | solution.py:21
  43.5 4.7 %gather_fusion = bf16[128,128,128]{2,1,0:T(8,128)(2,1)} fusion(bf16[64,128,128]{2,1,0:T(8,128)(2,1)} %get-tuple-element.226, s32[1024]{0:T(1024)S(1)} %pad_clamp_fusion.8), kind=kCustom, calls=%fused_computation.clone.1 | custom fusion | bytes 8389120 | tf_op jit(solution)/shard_map/while/body/eval_jaxpr/gather | solution.py:18
  48.2 3.0 gather_fusion.1
  51.2 8.2 %fusion.31 = f32[128,128,128]{2,1,0:T(8,128)} fusion(bf16[128,128,128]{2,1,0:T(8,128)(2,1)} %gather_fusion, bf16[128,128,128]{2,1,0:T(8,128)(2,1)} %gather_fusion.1), kind=kOutput, calls=%fused_computation.35.clone.1 | convolution fusion | flops 536870912 | bytes 16777216 | tf_op jit(solution)/shard_map/while/body/eval_jaxpr/gab,gae->gbe/dot_general | solution.py:20
  59.5 17.0 %scatter_fusion = f32[8,128,128]{2,1,0:T(8,128)S(1)} fusion(f32[8,128,128]{2,1,0:T(8,128)S(1)} %get-tuple-element.215, s32[128]{0:T(128)S(1)} %fusion.29, f32[128,128,128]{2,1,0:T(8,128)} %fusion.31), kind=kCustom, calls=%fused_computation.4.clone.1 | custom fusion | flops 2097152 | bytes 25166336 | tf_op jit(solution)/shard_map/while/body/eval_jaxpr/scatter-add | solution.py:21
  76.5 4.7 %gather_fusion = bf16[128,128,128]{2,1,0:T(8,128)(2,1)} fusion(bf16[64,128,128]{2,1,0:T(8,128)(2,1)} %get-tuple-element.226, s32[1024]{0:T(1024)S(1)} %pad_clamp_fusion.8), kind=kCustom, calls=%fused_computation.clone.1 | custom fusion | bytes 8389120 | tf_op jit(solution)/shard_map/while/body/eval_jaxpr/gather | solution.py:18
  81.2 3.0 gather_fusion.1
  84.2 8.2 %fusion.31 = f32[128,128,128]{2,1,0:T(8,128)} fusion(bf16[128,128,128]{2,1,0:T(8,128)(2,1)} %gather_fusion, bf16[128,128,128]{2,1,0:T(8,128)(2,1)} %gather_fusion.1), kind=kOutput, calls=%fused_computation.35.clone.1 | convolution fusion | flops 536870912 | bytes 16777216 | tf_op jit(solution)/shard_map/while/body/eval_jaxpr/gab,gae->gbe/dot_general | solution.py:20
  92.5 17.0 %scatter_fusion = f32[8,128,128]{2,1,0:T(8,128)S(1)} fusion(f32[8,128,128]{2,1,0:T(8,128)S(1)} %get-tuple-element.215, s32[128]{0:T(128)S(1)} %fusion.29, f32[128,128,128]{2,1,0:T(8,128)} %fusion.31), kind=kCustom, calls=%fused_computation.4.clone.1 | custom fusion | flops 2097152 | bytes 25166336 | tf_op jit(solution)/shard_map/while/body/eval_jaxpr/scatter-add | solution.py:21
  109.5 0.0 copy-start.1
  109.5 0.8 copy-done.1
  110.3 0.0 all-reduce.3.cloned.1.call-update
  110.3 0.0 all-reduce.5.cloned.1.call-start
  110.4 75.2 %all-reduce.3.cloned.1.call-done = f32[1024,128]{1,0:T(8,128)} async-done(((f32[1024,128]{1,0:T(8,128)}), f32[1024,128]{1,0:T(8,128)}) %all-reduce.3.cloned.1.call-update) | async-done | bytes 524304 | tf_op jit(solution)/shard_map/psum | solution.py:60
  185.5 0.0 copy-done.3
  185.5 1.1 fusion.10
  186.7 0.0 copy-start.2
  186.7 98.2 %while.21 = (s32[]{:T(128)}, f32[8,128,128]{2,1,0:T(8,128)S(1)}, s32[3,128]{1,0:T(4,128)S(1)}, s32[3,128]{1,0:T(4,128)S(1)}, bf16[64,128,128]{2,1,0:T(8,128)(2,1...) while((s32[]{:T(128)}, f32[8,128,128]{2,1,0:T(8,128)S(1)}, ...), condition=%wide.region_6.7_spmd, body=%wide.region_4.6_spmd.sunk | while | flops 538970880 | bytes 58734172 | solution.py:43
  186.8 4.7 %gather_fusion.2 = bf16[128,128,128]{2,1,0:T(8,128)(2,1)} fusion(bf16[64,128,128]{2,1,0:T(8,128)(2,1)} %get-tuple-element.250, s32[1024]{0:T(1024)S(1)} %pad_clamp_fusion.10), kind=kCustom, calls=%fused_computation.2.clone.1 | custom fusion | bytes 8389120 | tf_op jit(solution)/shard_map/while/body/eval_jaxpr/gather | solution.py:37
  191.5 3.0 gather_fusion.3
  194.5 7.9 %fusion.36 = f32[128,128,128]{2,1,0:T(8,128)} fusion(bf16[128,128,128]{2,1,0:T(8,128)(2,1)} %gather_fusion.2, bf16[128,128,128]{2,1,0:T(8,128)(2,1)} %gather_fusion.3), kind=kOutput, calls=%fused_computation.36.clone.1 | convolution fusion | flops 536870912 | bytes 16777216 | tf_op jit(solution)/shard_map/while/body/eval_jaxpr/gab,gbe->gae/dot_general | solution.py:39
  202.5 17.0 %scatter_fusion.1 = f32[8,128,128]{2,1,0:T(8,128)S(1)} fusion(f32[8,128,128]{2,1,0:T(8,128)S(1)} %get-tuple-element.239, s32[128]{0:T(128)S(1)} %fusion.34, f32[128,128,128]{2,1,0:T(8,128)} %fusion.36), kind=kCustom, calls=%fused_computation.5.clone.1 | custom fusion | flops 2097152 | bytes 25166336 | tf_op jit(solution)/shard_map/while/body/eval_jaxpr/scatter-add | solution.py:40
  219.5 4.7 %gather_fusion.2 = bf16[128,128,128]{2,1,0:T(8,128)(2,1)} fusion(bf16[64,128,128]{2,1,0:T(8,128)(2,1)} %get-tuple-element.250, s32[1024]{0:T(1024)S(1)} %pad_clamp_fusion.10), kind=kCustom, calls=%fused_computation.2.clone.1 | custom fusion | bytes 8389120 | tf_op jit(solution)/shard_map/while/body/eval_jaxpr/gather | solution.py:37
  224.2 3.0 gather_fusion.3
  227.2 7.9 %fusion.36 = f32[128,128,128]{2,1,0:T(8,128)} fusion(bf16[128,128,128]{2,1,0:T(8,128)(2,1)} %gather_fusion.2, bf16[128,128,128]{2,1,0:T(8,128)(2,1)} %gather_fusion.3), kind=kOutput, calls=%fused_computation.36.clone.1 | convolution fusion | flops 536870912 | bytes 16777216 | tf_op jit(solution)/shard_map/while/body/eval_jaxpr/gab,gbe->gae/dot_general | solution.py:39
  235.2 17.0 %scatter_fusion.1 = f32[8,128,128]{2,1,0:T(8,128)S(1)} fusion(f32[8,128,128]{2,1,0:T(8,128)S(1)} %get-tuple-element.239, s32[128]{0:T(128)S(1)} %fusion.34, f32[128,128,128]{2,1,0:T(8,128)} %fusion.36), kind=kCustom, calls=%fused_computation.5.clone.1 | custom fusion | flops 2097152 | bytes 25166336 | tf_op jit(solution)/shard_map/while/body/eval_jaxpr/scatter-add | solution.py:40
  252.2 4.7 %gather_fusion.2 = bf16[128,128,128]{2,1,0:T(8,128)(2,1)} fusion(bf16[64,128,128]{2,1,0:T(8,128)(2,1)} %get-tuple-element.250, s32[1024]{0:T(1024)S(1)} %pad_clamp_fusion.10), kind=kCustom, calls=%fused_computation.2.clone.1 | custom fusion | bytes 8389120 | tf_op jit(solution)/shard_map/while/body/eval_jaxpr/gather | solution.py:37
  256.9 3.0 gather_fusion.3
  259.9 7.9 %fusion.36 = f32[128,128,128]{2,1,0:T(8,128)} fusion(bf16[128,128,128]{2,1,0:T(8,128)(2,1)} %gather_fusion.2, bf16[128,128,128]{2,1,0:T(8,128)(2,1)} %gather_fusion.3), kind=kOutput, calls=%fused_computation.36.clone.1 | convolution fusion | flops 536870912 | bytes 16777216 | tf_op jit(solution)/shard_map/while/body/eval_jaxpr/gab,gbe->gae/dot_general | solution.py:39
  267.9 17.0 %scatter_fusion.1 = f32[8,128,128]{2,1,0:T(8,128)S(1)} fusion(f32[8,128,128]{2,1,0:T(8,128)S(1)} %get-tuple-element.239, s32[128]{0:T(128)S(1)} %fusion.34, f32[128,128,128]{2,1,0:T(8,128)} %fusion.36), kind=kCustom, calls=%fused_computation.5.clone.1 | custom fusion | flops 2097152 | bytes 25166336 | tf_op jit(solution)/shard_map/while/body/eval_jaxpr/scatter-add | solution.py:40
  284.9 0.0 copy-start
  284.9 0.8 copy-done
  285.7 0.0 all-reduce.5.cloned.1.call-update
  285.7 0.6 dynamic-slice_bitcast_fusion
  286.4 32.0 %all-reduce.5.cloned.1.call-done = f32[8,128,128]{2,1,0:T(8,128)} async-done(((f32[8,128,128]{2,1,0:T(8,128)}), f32[8,128,128]{2,1,0:T(8,128)}) %all-reduce.5.cloned.1.call-update) | async-done | bytes 524304 | tf_op jit(solution)/shard_map/psum | solution.py:68
  318.4 1.1 broadcast_multiply_fusion
  319.5 0.0 copy-done.2
  319.5 0.9 bitcast_add_fusion
  (26 shorter events, 0.2 us)
Async XLA Ops:
  7.2 178.3 %all-reduce.3.cloned.1.call-start = ((), (), s32[]{:S(2)}) async-start(), calls=%async_computation | async-start | bytes 1048576 | tf_op jit(solution)/shard_map/psum | solution.py:60
  10.4 175.1 %copy-start.3 = (f32[1,1024,128]{2,1,0:T(8,128)S(1)}, f32[1,1024,128]{2,1,0:T(8,128)}, u32[]{:S(2)}) copy-start(f32[1,1024,128]{2,1,0:T(8,128)} %param.11) | copy-start | bytes 1572868
  109.5 0.8 copy-start.1
  110.3 208.1 %all-reduce.5.cloned.1.call-start = ((), (), s32[]{:S(2)}) async-start(), calls=%async_computation.1 | async-start | bytes 1048576 | tf_op jit(solution)/shard_map/psum | solution.py:68
  186.7 132.8 %copy-start.2 = (f32[1024,128]{1,0:T(8,128)S(1)}, f32[1024,128]{1,0:T(8,128)}, u32[]{:S(2)}) copy-start(f32[1024,128]{1,0:T(8,128)} %param.10) | copy-start | bytes 1572868
  284.9 0.8 copy-start
Sparse Core Ops, SparseCore 0:
  110.4 75.0 all-reduce.2
  285.9 32.4 all-reduce.4
where the time goes:
time: 330 us; the launch traced here: 327 us
  other arithmetic  108 us (33%)
  waiting for transfers between devices  107 us (32%)
  local copies, waits for them, and re-layouts  48.6 us (15%)
  matrix products  48.5 us (15%)
  between operations  14.1 us (4%)
    psum x1, waiting for transfers between devices, per_device(): totals = lax.psum(partial_flat, 'users')  75.2 us
    scatter-add x3, other arithmetic, user_add_group(): jax.ops.segment_sum(products, lists[0], num_segments=n_tiles)  51.1 us
    scatter-add x3, other arithmetic, item_add_group(): jax.ops.segment_sum(products, lists[1], num_segments=n_items)  51.1 us
    psum x1, waiting for transfers between devices, per_device(): user_sum = lax.psum(user_part, 'panel')  32 us
    dot_general x3, matrix products, item_add_group(): jnp.einsum('gab,gae->gbe', tiles, rows, preferred_element_type=jnp.float32)  24.7 us
    dot_general x3, matrix products, user_add_group(): jnp.einsum('gab,gbe->gae', tiles, rows, preferred_element_type=jnp.float32)  23.8 us
    gather x3, local copies, waits for them, and re-layouts, user_add_group(): tiles = weight_tiles[lists[2]]  14 us
    gather x3, local copies, waits for them, and re-layouts, item_add_group(): tiles = weight_tiles[lists[2]]  14 us
  transfers between devices with their start and end apart: 2, of which 2 were waited for; matrix products, arithmetic and copies ran while one was open for 0% of the time, Pallas kernels for 0%

commit v1 on v0

v1 whole, which is shorter than its diff:
```python
import functools

import jax
import jax.numpy as jnp
from jax import lax
from jax.experimental import pallas as pl
from jax.experimental.pallas import tpu as pltpu
from jax.sharding import PartitionSpec as P

teleport = 0.2
ITEM_GROUP = 8
MESH = pl.DeviceIdType.MESH


def sum_weights(n_blocks, n_items, group, tile, users, items, weights, tiles, out, acc):
    n_user_tiles = out.shape[1] // tile
    first = pl.program_id(0) * group
    acc[...] = jnp.zeros_like(acc)

    def add(k, carry):
        i = items[k] - first

        def go():
            slot = i * n_user_tiles + users[k]
            acc[slot] += tiles[weights[k]].astype(jnp.float32)

        if group == n_items:
            go()
        else:
            pl.when((i >= 0) & (i < group))(go)
        return carry

    lax.fori_loop(0, n_blocks, add, 0, unroll=8)
    for i in range(group):
        for u in range(n_user_tiles):
            out[i, u * tile : (u + 1) * tile, :] = acc[i * n_user_tiles + u].astype(out.dtype)


def run(lo, hi, body):
    if hi - lo <= 8:
        for s in range(lo, hi):
            body(s)
    else:
        lax.fori_loop(lo, hi, lambda s, c: (body(s), c)[1], 0)


def exchange(
    n, tile, user, base, a, user_out, item_out,
    ut, total, sends, recvs, embs, part, core_send, core_recv, y_send, y_recv,
    s1, r1, s2, r2, s3, r3, s4, r4, s5, r5,
):
    me = lax.axis_index("users")
    panel = lax.axis_index("panel")
    core = lax.rem(panel, 2)
    other = panel + 1 - 2 * core
    across = lax.rem(panel + 2, 4)
    rows = user.shape[0]
    half = rows // 2
    chunks = half // tile

    barrier = pltpu.get_barrier_semaphore()

    def greet(s):
        pl.semaphore_signal(
            barrier, inc=1, device_id={"users": lax.rem(me + s, n), "panel": panel}, device_id_type=MESH
        )

    run(1, n, greet)
    for p in (other, across):
        pl.semaphore_signal(barrier, inc=1, device_id={"users": me, "panel": p}, device_id_type=MESH)

    ut[...] = jnp.transpose(user[...]).astype(ut.dtype)

    def term(t):
        return jnp.dot(ut[...], a[t], preferred_element_type=jnp.float32)

    total[...] = term(me)
    pl.semaphore_wait(barrier, n + 1)

    def to(s, src, dst, ssem, rsem):
        return pltpu.make_async_remote_copy(
            src_ref=src, dst_ref=dst, send_sem=ssem, recv_sem=rsem,
            device_id={"users": lax.rem(me + s, n), "panel": panel}, device_id_type=MESH,
        )

    def hop(p, src, dst, ssem, rsem):
        return pltpu.make_async_remote_copy(
            src_ref=src, dst_ref=dst, send_sem=ssem, recv_sem=rsem,
            device_id={"users": me, "panel": p}, device_id_type=MESH,
        )

    def partial(s):
        return to(s, sends.at[s], recvs.at[s], s1.at[s], r1.at[s])

    def send_partial(s):
        sends[s] = term(lax.rem(me + s, n)).astype(sends.dtype)
        partial(s).start()

    run(1, n, send_partial)

    def add_partial(s):
        partial(s).wait_recv()
        total[...] += recvs[s].astype(jnp.float32)

    run(1, n, add_partial)
    own = pl.ds(pl.multiple_of(me * tile, tile), tile)
    emb = (1.0 - teleport) * jnp.transpose(total[...]) + teleport * base[own, :]
    item_out[...] = emb
    embs[me] = emb.astype(embs.dtype)

    def spread(s):
        to(s, embs.at[me], embs.at[me], s2.at[s], r2.at[s]).start()

    run(1, n, spread)
    part[...] = jnp.dot(a[me], embs[me], preferred_element_type=jnp.float32)

    def use(s):
        j = lax.rem(me - s + n, n)
        to(s, embs.at[j], embs.at[j], s2.at[s], r2.at[s]).wait_recv()
        part[...] += jnp.dot(a[j], embs[j], preferred_element_type=jnp.float32)

    run(1, n, use)

    mine = core * half
    theirs = half - mine

    def to_core(k):
        return hop(other, core_send.at[k], core_recv.at[k], s3.at[k], r3.at[k])

    def to_y(k):
        return hop(across, y_send.at[k], y_recv.at[k], s4.at[k], r4.at[k])

    def back(k):
        where = pl.ds(pl.multiple_of(mine + k * tile, tile), tile)
        return hop(other, user_out.at[where, :], user_out.at[where, :], s5.at[k], r5.at[k])

    def back_recv(k):
        where = pl.ds(pl.multiple_of(theirs + k * tile, tile), tile)
        return hop(other, user_out.at[where, :], user_out.at[where, :], s5.at[k], r5.at[k])

    for k in range(chunks):
        core_send[k] = part[pl.ds(pl.multiple_of(theirs + k * tile, tile), tile), :].astype(core_send.dtype)
        to_core(k).start()
    for k in range(chunks):
        to_core(k).wait_recv()
        where = pl.ds(pl.multiple_of(mine + k * tile, tile), tile)
        y_send[k] = (part[where, :] + core_recv[k].astype(jnp.float32)).astype(y_send.dtype)
        to_y(k).start()
    for k in range(chunks):
        to_y(k).wait_recv()
        where = pl.ds(pl.multiple_of(mine + k * tile, tile), tile)
        both = y_send[k].astype(jnp.float32) + y_recv[k].astype(jnp.float32)
        user_out[where, :] = (1.0 - teleport) * both + teleport * user[where, :]
        back(k).start()

    def drain(s):
        partial(s).wait_send()
        to(s, embs.at[me], embs.at[me], s2.at[s], r2.at[s]).wait_send()

    run(1, n, drain)
    for k in range(chunks):
        to_core(k).wait_send()
        to_y(k).wait_send()
        back(k).wait_send()
        back_recv(k).wait_recv()


def per_device(user_emb0, item_base, weight_tiles, blk_user, blk_item, blk_weight):
    n = lax.axis_size("users")
    n_weights, tile, width = weight_tiles.shape[0], weight_tiles.shape[1], user_emb0.shape[1]
    rows = user_emb0.shape[0]
    n_user_tiles = rows // tile
    n_items = item_base.shape[1] // tile
    n_blocks = blk_user.shape[-1]
    group = min(n_items, ITEM_GROUP)
    smem = pl.BlockSpec(memory_space=pltpu.SMEM)
    vmem = pl.BlockSpec(memory_space=pltpu.VMEM)
    bf, f32 = jnp.bfloat16, jnp.float32
    dma = pltpu.SemaphoreType.DMA

    a = pl.pallas_call(
        functools.partial(sum_weights, n_blocks, n_items, group, tile),
        grid=(n_items // group,),
        out_shape=jax.ShapeDtypeStruct((n_items, rows, tile), bf),
        in_specs=[smem, smem, smem, vmem],
        out_specs=pl.BlockSpec((group, rows, tile), lambda g: (g, 0, 0)),
        scratch_shapes=[pltpu.VMEM((group * n_user_tiles, tile, tile), f32)],
        compiler_params=pltpu.CompilerParams(vmem_limit_bytes=24 << 20),
    )(blk_user.reshape(-1), blk_item.reshape(-1), blk_weight.reshape(-1), weight_tiles)

    chunks = rows // 2 // tile
    user_out, own = pl.pallas_call(
        functools.partial(exchange, n, tile),
        out_shape=(
            jax.ShapeDtypeStruct((rows, width), f32),
            jax.ShapeDtypeStruct((tile, width), f32),
        ),
        in_specs=[vmem] * 3,
        out_specs=(vmem, vmem),
        scratch_shapes=[
            pltpu.VMEM((width, rows), bf),
            pltpu.VMEM((width, tile), f32),
            pltpu.VMEM((n, width, tile), bf),
            pltpu.VMEM((n, width, tile), bf),
            pltpu.VMEM((n, tile, width), bf),
            pltpu.VMEM((rows, width), f32),
            pltpu.VMEM((chunks, tile, width), bf),
            pltpu.VMEM((chunks, tile, width), bf),
            pltpu.VMEM((chunks, tile, width), bf),
            pltpu.VMEM((chunks, tile, width), bf),
        ]
        + [dma((n,))] * 4
        + [dma((chunks,))] * 6,
        compiler_params=pltpu.CompilerParams(
            collective_id=0, has_side_effects=True, vmem_limit_bytes=48 << 20
        ),
    )(user_emb0, item_base[0], a)
    return user_out, own[None]


def solution(mesh):
    placed = (
        P("users", None),
        P("panel", None, None),
        P(),
        P("users", "panel", None),
        P("users", "panel", None),
        P("users", "panel", None),
    )
    return jax.shard_map(
        per_device,
        mesh=mesh,
        in_specs=placed,
        out_specs=(P("users", None), P("panel", "users", None)),
        check_vma=False,
    )
```

time: 330 us -> 37 us (0.11)
  waiting for transfers between devices: 107 us -> 0 us
  other arithmetic: 108 us -> 2.1 us
  matrix products: 48.5 us -> 0 us
  local copies, waits for them, and re-layouts: 48.6 us -> 3.02 us
  Pallas kernels: 0 us -> 31 us
  between operations: 14.1 us -> 0.67 us
    psum x2 -> x0, waiting for transfers between devices: 107 us -> none  [the longest x1 75.2 us: per_device(): totals = lax.psum(partial_flat, 'users')]
    scatter-add x6 -> x0, other arithmetic: 102 us -> none  [the longest x3 51.1 us: user_add_group(): jax.ops.segment_sum(products, lists[0], num_segments=n_tiles)]
    dot_general x6 -> x0, matrix products: 48.5 us -> none  [the longest x3 24.7 us: item_add_group(): jnp.einsum('gab,gae->gbe', tiles, rows, preferred_element_type=jnp.float32)]
    gather x12 -> x0, local copies, waits for them, and re-layouts: 46.3 us -> none  [the longest x3 14 us: user_add_group(): tiles = weight_tiles[lists[2]]]
    pallas_call x0 -> x2, Pallas kernels: none -> 31 us  [the longest x1 26.8 us: per_device(): pl.pallas_call(functools.partial(exchange, n, tile), out_shape=(jax.Shape...]
  transfers between devices with their start and end apart: 2 -> 0, of which waited for: 2 -> 0; matrix products, arithmetic and copies ran while one was open for 0% -> 0% of each run, Pallas kernels for 0% -> 0%
where the time goes in v1:
time: 37 us; the launch traced here: 36.8 us
  Pallas kernels  31 us (84%)
  local copies, waits for them, and re-layouts  3.02 us (8%)
  other arithmetic  2.1 us (6%)
  between operations  0.67 us (2%)
    pallas_call x1, Pallas kernels, per_device(): pl.pallas_call(functools.partial(exchange, n, tile), out_shape=(jax.Shape...  26.8 us
    pallas_call x1, Pallas kernels, per_device(): pl.pallas_call(functools.partial(sum_weights, n_blocks, n_items, group, t...  4.18 us
    unnamed x8, local copies, waits for them, and re-layouts  3.02 us
    unnamed x3, other arithmetic  2.1 us

profile of v1, /device:TPU:0, one launch (start us, length us, event | category | flops | bytes accessed | tf_op | source)
XLA Modules:
  0.0 36.8 jit_solution(3345090324097197205)
XLA Ops:
  0.6 0.7 %reduce.users = s32[384]{0:T(512)S(1)} reduce(s32[1,1,384]{2,1,0:T(1,128)} %param.9, s32[]{:T(128)} %constant.4), dimensions={0,1}, to_apply=%param.9.reduce_sub_computation | reduce | bytes 3076 | tf_op args[3]
  1.3 0.7 %reduce.1.items = s32[384]{0:T(512)S(1)} reduce(s32[1,1,384]{2,1,0:T(1,128)} %param.10, s32[]{:T(128)} %constant.4), dimensions={0,1}, to_apply=%param.10.reduce_sub_computation | reduce | bytes 3076 | tf_op args[4]
  2.0 0.7 %reduce.2.weights = s32[384]{0:T(512)S(1)} reduce(s32[1,1,384]{2,1,0:T(1,128)} %param.11, s32[]{:T(128)} %constant.4), dimensions={0,1}, to_apply=%param.11.reduce_sub_computation | reduce | bytes 3076 | tf_op args[5]
  2.7 0.0 copy-start
  2.7 1.6 %copy-done = bf16[64,128,128]{2,1,0:T(8,128)(2,1)S(1)} copy-done((bf16[64,128,128]{2,1,0:T(8,128)(2,1)S(1)}, bf16[64,128,128]{2,1,0:T(8,128)(2,1)}, u32[]{:S(2)}) %copy-start) | copy-done | bytes 2097176
  4.3 0.0 copy-start.1
  4.3 0.0 copy-start.2
  4.3 4.2 %shard_map.77.a = bf16[8,1024,128]{2,1,0:T(8,128)(2,1)S(1)} custom-call(s32[384]{0:T(512)S(1)} %reduce.users, s32[384]{0:T(512)S(1)} %reduce.1.items, s32[384]{0:T(512)S(1)} %reduce.2.weights, bf16[64,128,128]{2,1,0:T(8,128)(2,1)S(1)} %copy-done), custom_call_target="tpu_custom_call" | custom-call | tf_op jit(solution)/shard_map/pallas_call | solution.py:181
  8.5 0.0 copy-done.1
  8.5 0.0 copy-done.2
  8.5 26.8 %shard_map.78 = (f32[1024,128]{1,0:T(8,128)S(1)}, f32[128,128]{1,0:T(8,128)S(1)}) custom-call(f32[1024,128]{1,0:T(8,128)S(1)} %copy-done.1, f32[1024,128]{1,0:T(8,128)S(1)} %bitcast.2, bf16[8,1024,128]{2,1,0:T(8,128)(2,1)S(1)} %shard_map.77.a), custom_call_target="tpu_custom_call" | custom-call | tf_op jit(solution)/shard_map/pallas_call | solution.py:192
  35.4 0.8 %copy.10 = f32[1024,128]{1,0:T(8,128)} copy(f32[1024,128]{1,0:T(8,128)S(1)} %get-tuple-element.8) | data formatting | bytes 1048576
  36.2 0.6 %copy.11 = f32[1,128,128]{2,1,0:T(8,128)} copy(f32[1,128,128]{2,1,0:T(8,128)S(1)} %bitcast.3) | data formatting | bytes 131072
Async XLA Ops:
  2.7 1.6 %copy-start = (bf16[64,128,128]{2,1,0:T(8,128)(2,1)S(1)}, bf16[64,128,128]{2,1,0:T(8,128)(2,1)}, u32[]{:S(2)}) copy-start(bf16[64,128,128]{2,1,0:T(8,128)(2,1)} %tiles.1) | copy-start | bytes 6291460
  4.3 4.2 %copy-start.1 = (f32[1024,128]{1,0:T(8,128)S(1)}, f32[1024,128]{1,0:T(8,128)}, u32[]{:S(2)}) copy-start(f32[1024,128]{1,0:T(8,128)} %user.1) | copy-start | bytes 1572868
  4.3 4.2 %copy-start.2 = (f32[1,1024,128]{2,1,0:T(8,128)S(1)}, f32[1,1024,128]{2,1,0:T(8,128)}, u32[]{:S(2)}) copy-start(f32[1,1024,128]{2,1,0:T(8,128)} %param.7) | copy-start | bytes 1572868

commit v2 on v1

v2 whole, which is shorter than its diff:
```python
import functools

import jax
import jax.numpy as jnp
from jax import lax
from jax.experimental import pallas as pl
from jax.experimental.pallas import tpu as pltpu
from jax.sharding import PartitionSpec as P

teleport = 0.2
ITEM_GROUP = 8
HALVES = 1
CUTS = 2
MESH = pl.DeviceIdType.MESH


def sum_weights(n_blocks, n_items, group, tile, listed, tiles, out, acc):
    n_user_tiles = out.shape[1] // tile
    first = pl.program_id(0) * group
    acc[...] = jnp.zeros_like(acc)

    def add(k, carry):
        pair = lax.div(listed[k], tiles.shape[0])
        slot = pair - first * n_user_tiles
        w = listed[k] - pair * tiles.shape[0]

        def go():
            acc[slot] += tiles[w].astype(jnp.float32)

        if group == n_items:
            go()
        else:
            pl.when((slot >= 0) & (slot < group * n_user_tiles))(go)
        return carry

    lax.fori_loop(0, n_blocks, add, 0, unroll=8)
    for i in range(group):
        for u in range(n_user_tiles):
            out[i, u * tile : (u + 1) * tile, :] = acc[i * n_user_tiles + u].astype(out.dtype)


def run(lo, hi, body):
    if hi - lo <= 8:
        for s in range(lo, hi):
            body(s)
    else:
        lax.fori_loop(lo, hi, lambda s, c: (body(s), c)[1], 0)


def exchange(
    n, tile, user, base, a, user_out, item_out,
    ut, base_t, total, emb_t, sends, recvs, embs, part, core_send, core_recv, y_send, y_recv, done,
    s1, r1, s2, r2, s3, r3, s4, r4, s5, r5,
):
    me = lax.axis_index("users")
    panel = lax.axis_index("panel")
    core = lax.rem(panel, 2)
    other = panel + 1 - 2 * core
    across = lax.rem(panel + 2, 4)
    cuts, cols = part.shape[1], part.shape[3]
    half = cuts * cols
    depth = total.shape[0] // HALVES

    def peer(s):
        return {"users": lax.rem(me + s, n), "panel": panel}

    def hop(where, src, dst, ssem, rsem):
        return pltpu.make_async_remote_copy(
            src_ref=src, dst_ref=dst, send_sem=ssem, recv_sem=rsem, device_id=where, device_id_type=MESH
        )

    barrier = pltpu.get_barrier_semaphore()

    def greet(where):
        pl.semaphore_signal(barrier, inc=1, device_id=where, device_id_type=MESH)

    run(1, n, lambda s: greet(peer(s)))
    greet({"users": me, "panel": other})
    greet({"users": me, "panel": across})

    ut[...] = jnp.transpose(user[...]).astype(ut.dtype)
    own = pl.ds(pl.multiple_of(me * tile, tile), tile)
    base_t[...] = teleport * jnp.transpose(base[own, :])

    def term(t):
        return jnp.dot(ut[...], a[t], preferred_element_type=jnp.float32)

    total[...] = term(me)
    pl.semaphore_wait(barrier, n + 1)

    def deep(h):
        return pl.ds(h * depth, depth)

    def partial(h, s):
        return hop(peer(s), sends.at[s, deep(h)], recvs.at[s, deep(h)], s1.at[h, s], r1.at[h, s])

    def spread(h, s, j):
        return hop(peer(s), embs.at[j, deep(h)], embs.at[j, deep(h)], s2.at[h, s], r2.at[h, s])

    def send_partial(s):
        sends[s] = term(lax.rem(me + s, n)).astype(sends.dtype)
        partial(0, s).start()

    run(1, n, send_partial)
    for h in range(1, HALVES):
        run(1, n, lambda s: partial(h, s).start())

    def finish_items(h):
        def add_partial(s):
            partial(h, s).wait_recv()
            total[deep(h), :] += recvs[s, deep(h), :].astype(jnp.float32)

        run(1, n, add_partial)
        emb = (1.0 - teleport) * total[deep(h), :] + base_t[deep(h), :]
        emb_t[deep(h), :] = emb
        embs[me, deep(h), :] = emb.astype(embs.dtype)
        run(1, n, lambda s: spread(h, s, me).start())

    def multiply(h, j, first):
        for c in range(2):
            for k in range(cuts):
                rows = pl.ds(c * half + k * cols, cols)
                value = lax.dot_general(
                    embs[j, deep(h), :], a[j, rows, :], (((1,), (1,)), ((), ())),
                    preferred_element_type=jnp.float32,
                )
                part[c, k, deep(h), :] = value if first else part[c, k, deep(h), :] + value

    def use(h, lo, hi):
        def one(s):
            j = lax.rem(me - s + n, n)
            spread(h, s, j).wait_recv()
            multiply(h, j, False)

        run(lo, hi, one)

    def to_core(h, k):
        return hop({"users": me, "panel": other}, core_send.at[h, k], core_recv.at[h, k], s3.at[h, k], r3.at[h, k])

    def to_y(h, k):
        return hop({"users": me, "panel": across}, y_send.at[h, k], y_recv.at[h, k], s4.at[h, k], r4.at[h, k])

    def back(h, k, c):
        where = done.at[c, k, deep(h)]
        return hop({"users": me, "panel": other}, where, where, s5.at[h, k], r5.at[h, k])

    def give_core(h):
        for k in range(cuts):
            core_send[h, k] = part[1 - core, k, deep(h), :].astype(core_send.dtype)
            to_core(h, k).start()

    def give_y(h):
        for k in range(cuts):
            to_core(h, k).wait_recv()
            both = part[core, k, deep(h), :] + core_recv[h, k].astype(jnp.float32)
            y_send[h, k] = both.astype(y_send.dtype)
            to_y(h, k).start()

    def give_back(h):
        for k in range(cuts):
            to_y(h, k).wait_recv()
            done[core, k, deep(h), :] = y_send[h, k].astype(jnp.float32) + y_recv[h, k].astype(jnp.float32)
            back(h, k, core).start()

    def write(c, k):
        where = pl.ds(pl.multiple_of(c * half + k * cols, cols), cols)
        user_out[where, :] = (1.0 - teleport) * jnp.transpose(done[c, k]) + teleport * user[where, :]

    finish_items(0)
    multiply(0, me, True)
    item_out[...] = jnp.transpose(emb_t[...])
    use(0, 1, n)
    give_core(0)
    give_y(0)
    give_back(0)
    for k in range(cuts):
        write(core, k)

    def drain(s):
        for h in range(HALVES):
            partial(h, s).wait_send()
            spread(h, s, me).wait_send()

    run(1, n, drain)
    for k in range(cuts):
        for h in range(HALVES):
            to_core(h, k).wait_send()
            to_y(h, k).wait_send()
            back(h, k, core).wait_send()
            back(h, k, 1 - core).wait_recv()
        write(1 - core, k)


def per_device(user_emb0, item_base, weight_tiles, blk_user, blk_item, blk_weight):
    n = lax.axis_size("users")
    n_weights, tile, width = weight_tiles.shape[0], weight_tiles.shape[1], user_emb0.shape[1]
    rows = user_emb0.shape[0]
    n_user_tiles = rows // tile
    n_items = item_base.shape[1] // tile
    n_blocks = blk_user.shape[-1]
    group = min(n_items, ITEM_GROUP)
    smem = pl.BlockSpec(memory_space=pltpu.SMEM)
    vmem = pl.BlockSpec(memory_space=pltpu.VMEM)
    bf, f32 = jnp.bfloat16, jnp.float32
    dma = pltpu.SemaphoreType.DMA

    a = pl.pallas_call(
        functools.partial(sum_weights, n_blocks, n_items, group, tile),
        grid=(n_items // group,),
        out_shape=jax.ShapeDtypeStruct((n_items, rows, tile), bf),
        in_specs=[smem, vmem],
        out_specs=pl.BlockSpec((group, rows, tile), lambda g: (g, 0, 0)),
        scratch_shapes=[pltpu.VMEM((group * n_user_tiles, tile, tile), f32)],
        compiler_params=pltpu.CompilerParams(vmem_limit_bytes=24 << 20),
    )(((blk_item * n_user_tiles + blk_user) * n_weights + blk_weight).reshape(-1), weight_tiles)

    cols = rows // 2 // CUTS
    user_out, own = pl.pallas_call(
        functools.partial(exchange, n, tile),
        out_shape=(
            jax.ShapeDtypeStruct((rows, width), f32),
            jax.ShapeDtypeStruct((tile, width), f32),
        ),
        in_specs=[vmem] * 3,
        out_specs=(vmem, vmem),
        scratch_shapes=[
            pltpu.VMEM((width, rows), bf),
            pltpu.VMEM((width, tile), f32),
            pltpu.VMEM((width, tile), f32),
            pltpu.VMEM((width, tile), f32),
            pltpu.VMEM((n, width, tile), bf),
            pltpu.VMEM((n, width, tile), bf),
            pltpu.VMEM((n, width, tile), bf),
            pltpu.VMEM((2, CUTS, width, cols), f32),
        ]
        + [pltpu.VMEM((HALVES, CUTS, width // HALVES, cols), bf)] * 4
        + [pltpu.VMEM((2, CUTS, width, cols), f32)]
        + [dma((HALVES, n))] * 4
        + [dma((HALVES, CUTS))] * 6,
        compiler_params=pltpu.CompilerParams(
            collective_id=0, has_side_effects=True, vmem_limit_bytes=48 << 20
        ),
    )(user_emb0, item_base[0], a)
    return user_out, own[None]


def solution(mesh):
    placed = (
        P("users", None),
        P("panel", None, None),
        P(),
        P("users", "panel", None),
        P("users", "panel", None),
        P("users", "panel", None),
    )
    return jax.shard_map(
        per_device,
        mesh=mesh,
        in_specs=placed,
        out_specs=(P("users", None), P("panel", "users", None)),
        check_vma=False,
    )
```

time: 37 us -> 35.3 us (0.954)
  other arithmetic: 2.1 us -> 0.73 us
    unnamed x3 -> x0, other arithmetic: 2.1 us -> none
    add x0 -> x1, other arithmetic: none -> 0.73 us  [per_device(): (blk_item * n_user_tiles + blk_user) * n_weights + blk_weight]
where the time goes in v2:
time: 35.3 us; the launch traced here: 35.2 us
  Pallas kernels  30.7 us (87%)
  local copies, waits for them, and re-layouts  3.02 us (9%)
  other arithmetic  0.73 us (2%)
  between operations  0.67 us (2%)
    pallas_call x1, Pallas kernels, per_device(): pl.pallas_call(functools.partial(exchange, n, tile), out_shape=(jax.Shape...  26.5 us
    pallas_call x1, Pallas kernels, per_device(): pl.pallas_call(functools.partial(sum_weights, n_blocks, n_items, group, t...  4.21 us
    unnamed x8, local copies, waits for them, and re-layouts  3.02 us
    add x1, other arithmetic, per_device(): (blk_item * n_user_tiles + blk_user) * n_weights + blk_weight  0.73 us

profile of v2, /device:TPU:0, one launch (start us, length us, event | category | flops | bytes accessed | tf_op | source)
XLA Modules:
  0.0 35.2 jit_solution(6430369274554124040)
XLA Ops:
  0.6 0.7 %add_reduce_fusion.listed = s32[384]{0:T(512)S(1)} fusion(s32[1,1,384]{2,1,0:T(1,128)} %param.11, s32[1,1,384]{2,1,0:T(1,128)} %param.9, s32[1,1,384]{2,1,0:T(1,128)} %param.10), kind=kLoop, calls=%fused_computation | loop fusion | flops 1536 | bytes 6144 | tf_op jit(solution)/shard_map/add | solution.py:215
  1.4 0.0 copy-start
  1.4 1.6 %copy-done = bf16[64,128,128]{2,1,0:T(8,128)(2,1)S(1)} copy-done((bf16[64,128,128]{2,1,0:T(8,128)(2,1)S(1)}, bf16[64,128,128]{2,1,0:T(8,128)(2,1)}, u32[]{:S(2)}) %copy-start) | copy-done | bytes 2097176
  3.0 0.0 copy-start.1
  3.0 0.0 copy-start.2
  3.0 4.2 %shard_map.77.a = bf16[8,1024,128]{2,1,0:T(8,128)(2,1)S(1)} custom-call(s32[384]{0:T(512)S(1)} %add_reduce_fusion.listed, bf16[64,128,128]{2,1,0:T(8,128)(2,1)S(1)} %copy-done), custom_call_target="tpu_custom_call" | custom-call | tf_op jit(solution)/shard_map/pallas_call | solution.py:207
  7.2 0.0 copy-done.1
  7.2 0.0 copy-done.2
  7.2 26.5 %shard_map.78 = (f32[1024,128]{1,0:T(8,128)S(1)}, f32[128,128]{1,0:T(8,128)S(1)}) custom-call(f32[1024,128]{1,0:T(8,128)S(1)} %copy-done.1, f32[1024,128]{1,0:T(8,128)S(1)} %bitcast.2, bf16[8,1024,128]{2,1,0:T(8,128)(2,1)S(1)} %shard_map.77.a), custom_call_target="tpu_custom_call" | custom-call | tf_op jit(solution)/shard_map/pallas_call | solution.py:218
  33.7 0.8 %copy.10 = f32[1024,128]{1,0:T(8,128)} copy(f32[1024,128]{1,0:T(8,128)S(1)} %get-tuple-element.8) | data formatting | bytes 1048576
  34.5 0.6 %copy.11 = f32[1,128,128]{2,1,0:T(8,128)} copy(f32[1,128,128]{2,1,0:T(8,128)S(1)} %bitcast.3) | data formatting | bytes 131072
Async XLA Ops:
  1.4 1.6 %copy-start = (bf16[64,128,128]{2,1,0:T(8,128)(2,1)S(1)}, bf16[64,128,128]{2,1,0:T(8,128)(2,1)}, u32[]{:S(2)}) copy-start(bf16[64,128,128]{2,1,0:T(8,128)(2,1)} %tiles.1) | copy-start | bytes 6291460
  3.0 4.2 %copy-start.1 = (f32[1024,128]{1,0:T(8,128)S(1)}, f32[1024,128]{1,0:T(8,128)}, u32[]{:S(2)}) copy-start(f32[1024,128]{1,0:T(8,128)} %user.1) | copy-start | bytes 1572868
  3.0 4.2 %copy-start.2 = (f32[1,1024,128]{2,1,0:T(8,128)S(1)}, f32[1,1024,128]{2,1,0:T(8,128)}, u32[]{:S(2)}) copy-start(f32[1,1024,128]{2,1,0:T(8,128)} %param.7) | copy-start | bytes 1572868
